TPU v7x, 256 devices: a whole 4x4x8 slice. The times are simulated.
256 devices in a mesh: blk: 16 (over z, core), grp: 16 (over x, y).
Axes of the slice: x: 4, y: 4, z: 8, core: 2. Of those that a mesh axis runs over, the one named last changes fastest.
Arguments:
- queries: bfloat16 [256, 5120], P(('grp', 'blk')), parts along dimension 0, may hold values from -28 to 28
- cache_keys: bfloat16 [2048, 128, 1024], P(('grp', 'blk')), parts along dimension 0, may hold values from -24 to 24
- pool_values_prior: bfloat16 [2048, 128, 1024], P(('grp', 'blk')), parts along dimension 0, may hold values from -6 to 6
- prefill_keys: bfloat16 [512, 128, 1024], P(('grp', 'blk')), parts along dimension 0, may hold values from -6 to 6
- prefill_values: bfloat16 [512, 128, 1024], P(('grp', 'blk')), parts along dimension 0, may hold values from -6 to 6
- context_lengths: int32 [64], P('grp'), parts along dimension 0, may hold values from 1028 to 4096, as said below
- block_table: int32 [64, 32], P('grp'), parts along dimension 0, may hold values from 0 to 127, as said below
- spill_slots: int32 [512], P('grp'), parts along dimension 0, may hold values from 0 to 127, as said below
Outputs:
- attended: bfloat16 [256, 5120], P(('grp', 'blk')), parts along dimension 0
- pool_keys: bfloat16 [2048, 128, 1024], P(('grp', 'blk')), parts along dimension 0
- pool_values: bfloat16 [2048, 128, 1024], P(('grp', 'blk')), parts along dimension 0
There are 16 independent parts, one for each index of `grp`. A program takes and returns all parts, laid end to end along the dimension named above; each array names one. Nothing has to cross between parts.
Inputs may be any that keep to these rules, and one draw needn't show every extreme that they name: Every pool block appears exactly once in block_table, so each request owns 32 blocks. `spill_slots`: distinct pool blocks; exactly 2 of them lie in each rank's range of 8 blocks, and each stands among the first 8 columns of some row of block_table. `context_lengths`: some request has 4096 tokens.
All inputs are finite; a program needn't handle non-finite values.
Results may differ from a plain program's by a relative error of at most 0.0045.
Values may be sent and summed in bfloat16 or wider, within the bound.
No kernel may reach another device: no remote copies, remote signals or barrier semaphores. Data moves between devices by JAX's collectives and lax.ppermute only.
A program may use at most 128 MiB of HBM per device.

v0:
```python
import jax
import jax.numpy as jnp
from jax import lax
from jax.sharding import PartitionSpec as P

QUERY_HEADS = 40
KEY_VALUE_HEADS = 8
HEAD_SIZE = 128
STEPS = 4
REQ = 4


NEGATIVE_LARGE = -1e30


def shifted(value, axis, steps):
    count = lax.axis_size(axis)
    pairs = [(source, (source + steps) % count) for source in range(count)]
    return lax.ppermute(value, axis, pairs)


def merge_state(running, incoming):
    run_max, run_sum, run_out = running
    new_max, new_sum, new_out = incoming
    largest = jnp.maximum(run_max, new_max)
    keep = jnp.exp(run_max - largest)
    take = jnp.exp(new_max - largest)
    return (
        largest,
        run_sum * keep + new_sum * take,
        run_out * keep[..., None] + new_out * take[..., None],
    )


def local_partial(decode_query_rows, first_row, owner, limit, keys_of_block, values_of_block):
    block_count, query_width = decode_query_rows.shape
    rank_slots, block_index, width = keys_of_block.shape
    head_groups = QUERY_HEADS // KEY_VALUE_HEADS
    row_ids = first_row + jnp.arange(block_count, dtype=jnp.int32)
    step_of = row_ids // REQ
    request_of = row_ids % REQ
    query_head_rows = decode_query_rows.reshape(
        block_count, KEY_VALUE_HEADS, head_groups, HEAD_SIZE
    )
    key_head_rows = keys_of_block.reshape(rank_slots, block_index, KEY_VALUE_HEADS, HEAD_SIZE)
    scores = jnp.einsum(
        "rhgd,sthd->rhgst", query_head_rows, key_head_rows, preferred_element_type=jnp.float32
    ) * HEAD_SIZE ** (-0.5)
    bound = limit[None, :] - (STEPS - 1) + step_of[:, None]
    visible = jnp.arange(block_index, dtype=jnp.int32)[None, None, :] < bound[:, :, None]
    visible = visible & (owner[None, :] == request_of[:, None])[:, :, None]
    visible = visible[:, None, None]
    masked = jnp.where(visible, scores, NEGATIVE_LARGE)
    row_max = jnp.max(masked, axis=(-2, -1))
    weights = jnp.where(visible, jnp.exp(masked - row_max[..., None, None]), 0.0)
    row_sum = jnp.sum(weights, axis=(-2, -1))
    probs = weights.astype(jnp.bfloat16)
    value_head_rows = values_of_block.reshape(rank_slots, block_index, KEY_VALUE_HEADS, HEAD_SIZE)
    row_out = jnp.einsum(
        "rhgst,sthd->rhgd", probs, value_head_rows, preferred_element_type=jnp.float32
    )
    return (row_max, row_sum, row_out)


def per_device(
    queries,
    cache_keys,
    pool_values_prior,
    prefill_keys,
    prefill_values,
    context_lengths,
    block_table,
    spill_slots,
):
    ranks = lax.axis_size("blk")
    myself = lax.axis_index("blk")
    rank_slots, block_index, width = cache_keys.shape
    per_rank = prefill_keys.shape[0]
    total_spill = spill_slots.shape[0]
    local_first = myself * rank_slots
    target_rank = spill_slots // rank_slots
    sequence = jnp.arange(total_spill, dtype=jnp.int32)
    mine = target_rank == myself
    landing_all = spill_slots - local_first
    placing_ids = jnp.arange(rank_slots, dtype=jnp.int32)
    source_rank = sequence // per_rank
    same_pair = (target_rank[None, :] == target_rank[:, None]) & (
        source_rank[None, :] == source_rank[:, None]
    )
    order = jnp.sum((same_pair & (sequence[None, :] < sequence[:, None])).astype(jnp.int32), axis=1)
    own_target = lax.dynamic_slice_in_dim(target_rank, myself * per_rank, per_rank, 0)
    own_order = lax.dynamic_slice_in_dim(order, myself * per_rank, per_rank, 0)
    peers = jnp.arange(ranks, dtype=jnp.int32)
    lanes = jnp.arange(per_rank, dtype=jnp.int32)
    sending = (peers[:, None, None] == own_target[None, None, :]) & (
        lanes[None, :, None] == own_order[None, None, :]
    )
    sending_bf = sending.astype(jnp.bfloat16)
    send_keys = jnp.einsum(
        "dqb,btw->dqtw", sending_bf, prefill_keys, preferred_element_type=jnp.float32
    ).astype(jnp.bfloat16)
    send_values = jnp.einsum(
        "dqb,btw->dqtw", sending_bf, prefill_values, preferred_element_type=jnp.float32
    ).astype(jnp.bfloat16)
    got_keys, got_values = (
        lax.all_to_all(send_keys, "blk", split_axis=0, concat_axis=0, tiled=True),
        lax.all_to_all(send_values, "blk", split_axis=0, concat_axis=0, tiled=True),
    )
    got_keys = got_keys.reshape(ranks * per_rank, block_index, width)
    got_values = got_values.reshape(ranks * per_rank, block_index, width)
    position = source_rank * per_rank + order
    columns = jnp.arange(ranks * per_rank, dtype=jnp.int32)
    hit = (
        mine[None, None, :]
        & (placing_ids[:, None, None] == landing_all[None, None, :])
        & (columns[None, :, None] == position[None, None, :])
    )
    placing = jnp.any(hit, axis=2)
    arrived_keys, arrived_values = (got_keys, got_values)
    filled = jnp.any(placing, axis=1)[:, None, None]
    placing_bf = placing.astype(jnp.bfloat16)
    placed_keys = jnp.einsum(
        "sk,ktw->stw", placing_bf, arrived_keys, preferred_element_type=jnp.float32
    ).astype(jnp.bfloat16)
    placed_values = jnp.einsum(
        "sk,ktw->stw", placing_bf, arrived_values, preferred_element_type=jnp.float32
    ).astype(jnp.bfloat16)
    pool_keys = jnp.where(filled, placed_keys, cache_keys)
    pool_values = jnp.where(filled, placed_values, pool_values_prior)
    local_ids = local_first + jnp.arange(rank_slots, dtype=jnp.int32)
    matches = block_table[:, :, None] == local_ids[None, None, :]
    request_ids = jnp.arange(block_table.shape[0], dtype=jnp.int32)[:, None, None]
    owner = jnp.sum(jnp.where(matches, request_ids, 0), axis=(0, 1))
    columns_t = jnp.arange(block_table.shape[1], dtype=jnp.int32)[None, :, None]
    limit = jnp.sum(
        jnp.where(matches, context_lengths[:, None, None] - columns_t * block_index, 0), axis=(0, 1)
    )
    rank_block_count, query_width = queries.shape
    head_groups = QUERY_HEADS // KEY_VALUE_HEADS
    starting = (
        jnp.full((rank_block_count, KEY_VALUE_HEADS, head_groups), NEGATIVE_LARGE, jnp.float32),
        jnp.zeros((rank_block_count, KEY_VALUE_HEADS, head_groups), jnp.float32),
        jnp.zeros((rank_block_count, KEY_VALUE_HEADS, head_groups, HEAD_SIZE), jnp.float32),
    )

    def advance(index, carried):
        visiting, running = carried
        anchor = (myself - index) % ranks
        running = merge_state(
            running,
            local_partial(
                visiting, anchor * rank_block_count, owner, limit, pool_keys, pool_values
            ),
        )
        visiting = shifted(visiting, "blk", 1)
        running = shifted((running[0], running[1], running[2]), "blk", 1)
        return (visiting, running)

    finished, running = lax.fori_loop(0, ranks, advance, (queries, starting))
    totals = running[1]
    outputs = running[2]
    attended = outputs / totals[..., None]
    attended = attended.reshape(rank_block_count, query_width).astype(jnp.bfloat16)
    return (attended, pool_keys, pool_values)


def solution(mesh):
    placed = (
        P(("grp", "blk"), None),
        P(("grp", "blk"), None, None),
        P(("grp", "blk"), None, None),
        P(("grp", "blk"), None, None),
        P(("grp", "blk"), None, None),
        P("grp"),
        P("grp", None),
        P("grp"),
    )
    return jax.shard_map(
        per_device,
        mesh=mesh,
        in_specs=placed,
        out_specs=(
            P(("grp", "blk"), None),
            P(("grp", "blk"), None, None),
            P(("grp", "blk"), None, None),
        ),
        check_vma=False,
    )
```

profile of v0, /device:TPU:1, one launch (start us, length us, event | category | flops | bytes accessed | tf_op | source)
XLA Modules:
  0.0 551.4 jit_solution(15191035816195992887)
XLA Ops:
  1.7 5.8 %convolution_convert_fusion.1 = bf16[16,2,128,1024]{3,0,2,1:T(8,128)(2,1)} fusion(bf16[2,128,1024]{2,1,0:T(8,128)(2,1)} %param.13, pred[2,2]{1,0:T(4,128)(4,1)S(1)} %iota_compare_fusion.4, pred[16,2]{0,1:T(4,128)(4,1)S(1)} %iota_compare_fusion.5), kind=kOutput, calls=%fused_computation.40 | convolution fusion | flops 20971584 | bytes 8912932 | tf_op jit(solution)/shard_map/dqb,btw->dqtw/dot_general | solution.py:99
  7.6 11.3 %copy.52 = bf16[16,2,128,1024]{3,2,1,0:T(8,128)(2,1)} copy(bf16[16,2,128,1024]{3,0,2,1:T(8,128)(2,1)} %convolution_convert_fusion.1) | data formatting | bytes 16777216 | tf_op jit(solution)/shard_map/convert_element_type | solution.py:101
  18.9 10.8 %all-to-all-start = ((bf16[16,2,128,1024]{3,2,1,0:T(8,128)(2,1)}), bf16[16,2,128,1024]{3,2,1,0:T(8,128)(2,1)}, u32[]{:S(2)}, u32[]{:S(2)}) async-start(bf16[16,2,128,1024]{3,2,1,0:T(8,128)(2,1)} %copy.52), calls=%async_computation | async-start | bytes 16777216 | tf_op jit(solution)/shard_map/all_to_all | solution.py:106
  29.7 5.2 convolution_convert_fusion
  34.9 11.3 %copy.56 = bf16[16,2,128,1024]{3,2,1,0:T(8,128)(2,1)} copy(bf16[16,2,128,1024]{3,0,2,1:T(8,128)(2,1)} %convolution_convert_fusion) | data formatting | bytes 16777216 | tf_op jit(solution)/shard_map/convert_element_type | solution.py:104
  46.2 166.8 %all-to-all-done = bf16[16,2,128,1024]{3,2,1,0:T(8,128)(2,1)} async-done(((bf16[16,2,128,1024]{3,2,1,0:T(8,128)(2,1)}), bf16[16,2,128,1024]{3,2,1,0:T(8,128)(2,1)}, u32[]{:S(2)}, u32[]{:S(2)}) %all-to-all-start) | async-done | bytes 8388640 | tf_op jit(solution)/shard_map/all_to_all | solution.py:106
  213.0 5.6 %all-to-all-start.1 = ((bf16[16,2,128,1024]{3,2,1,0:T(8,128)(2,1)}), bf16[16,2,128,1024]{3,2,1,0:T(8,128)(2,1)}, u32[]{:S(2)}, u32[]{:S(2)}) async-start(bf16[16,2,128,1024]{3,2,1,0:T(8,128)(2,1)} %copy.56), calls=%async_computation.1 | async-start | bytes 16777216 | tf_op jit(solution)/shard_map/all_to_all | solution.py:107
  219.4 14.3 %copy_select_fusion.1 = bf16[8,128,1024]{2,0,1:T(8,128)(2,1)S(1)} fusion(bf16[8,128,1024]{2,1,0:T(8,128)(2,1)S(1)} %copy-done.1, pred[8]{0:T(512)(128)(4,1)S(1)} %get-tuple-element.342, bf16[32,128,1024]{2,1,0:T(8,128)(2,1)} %bitcast.20, pred[8,32]{1,0:T(8,128)(4,1)S(1)} %get-tuple-element.341), kind=kOutput, calls=%fused_computation.42 | convolution fusion | flops 69206016 | bytes 12583176 | tf_op jit(solution)/shard_map/sk,ktw->stw/dot_general | solution.py:122
  233.7 2.7 copy.59
  236.4 165.6 %all-to-all-done.1 = bf16[16,2,128,1024]{3,2,1,0:T(8,128)(2,1)} async-done(((bf16[16,2,128,1024]{3,2,1,0:T(8,128)(2,1)}), bf16[16,2,128,1024]{3,2,1,0:T(8,128)(2,1)}, u32[]{:S(2)}, u32[]{:S(2)}) %all-to-all-start.1) | async-done | bytes 8388640 | tf_op jit(solution)/shard_map/all_to_all | solution.py:107
  402.0 14.6 %copy_select_fusion = bf16[8,128,1024]{2,0,1:T(8,128)(2,1)S(1)} fusion(bf16[8,128,1024]{2,1,0:T(8,128)(2,1)S(1)} %copy-done.2, pred[8]{0:T(512)(128)(4,1)S(1)} %get-tuple-element.342, bf16[32,128,1024]{2,1,0:T(8,128)(2,1)} %bitcast.23, pred[8,32]{1,0:T(8,128)(4,1)S(1)} %get-tuple-element.341), kind=kOutput, calls=%fused_computation.41 | convolution fusion | flops 69206016 | bytes 12583176 | tf_op jit(solution)/shard_map/sk,ktw->stw/dot_general | solution.py:125
  417.8 131.9 %while.22 = (s32[]{:T(128)}, bf16[1,5120]{1,0:T(2,128)(2,1)S(1)}, f32[1,8,5]{2,1,0:T(8,128)S(1)}, f32[1,8,5]{2,1,0:T(8,128)S(1)}, f32[1,8,5,128]{3,2,1,0:T(8,128...) while((s32[]{:T(128)}, bf16[1,5120]{1,0:T(2,128)(2,1)S(1)}, ...), condition=%wide.region_8.9_spmd, body=%wide.region_5.8_spmd.sunk | while | flops 21357784 | bytes 4929771 | solution.py:159
  418.1 2.3 fusion.87
  424.7 2.3 fusion.87
  427.8 2.5 collective-permute-start.3
  475.6 2.3 fusion.87
  483.8 2.3 fusion.87
  492.1 2.3 fusion.87
  500.4 2.3 fusion.87
  508.6 2.3 fusion.87
  516.9 2.3 fusion.87
  525.2 2.3 fusion.87
  533.4 2.3 fusion.87
  541.7 2.3 fusion.87
  (314 shorter events, 107.3 us)
Async XLA Ops:
  18.9 194.2 %all-to-all-start = ((bf16[16,2,128,1024]{3,2,1,0:T(8,128)(2,1)}), bf16[16,2,128,1024]{3,2,1,0:T(8,128)(2,1)}, u32[]{:S(2)}, u32[]{:S(2)}) async-start(bf16[16,2,128,1024]{3,2,1,0:T(8,128)(2,1)} %copy.52), calls=%async_computation | async-start | bytes 16777216 | tf_op jit(solution)/shard_map/all_to_all | solution.py:106
  213.0 189.0 %all-to-all-start.1 = ((bf16[16,2,128,1024]{3,2,1,0:T(8,128)(2,1)}), bf16[16,2,128,1024]{3,2,1,0:T(8,128)(2,1)}, u32[]{:S(2)}, u32[]{:S(2)}) async-start(bf16[16,2,128,1024]{3,2,1,0:T(8,128)(2,1)} %copy.56), calls=%async_computation.1 | async-start | bytes 16777216 | tf_op jit(solution)/shard_map/all_to_all | solution.py:107
  421.2 3.2 collective-permute-start.3
  427.8 6.0 %collective-permute-start.3 = (f32[1,8,5,128]{3,2,1,0:T(8,128)S(1)}, f32[1,8,5,128]{3,2,1,0:T(8,128)S(1)}, u32[]{:S(2)}, u32[]{:S(2)}) collective-permute-start(f32[1,8,5,128]{3,2,1,0:T(8,128)S(1)} %fusion.90), channel_id=1, source_target_pairs={{0,16},{16,32},{32,48},{48,64},{64,80},{80,96},{96,112},{112,128},... | collective-permute-start | bytes 61448 | tf_op jit(solution)/shard_map/while/body/eval_jaxpr/ppermute | solution.py:19
  430.4 3.5 collective-permute-start
  437.2 4.5 collective-permute-start.3
  445.1 5.4 collective-permute-start.3
  447.4 3.2 collective-permute-start
  453.9 4.9 collective-permute-start.3
  455.9 3.0 collective-permute-start
  462.2 4.9 collective-permute-start.3
  464.1 3.0 collective-permute-start
  470.4 4.9 collective-permute-start.3
  472.4 3.0 collective-permute-start
  478.7 4.9 collective-permute-start.3
  480.7 3.0 collective-permute-start
  487.0 4.9 collective-permute-start.3
  495.3 4.9 collective-permute-start.3
  503.5 4.9 collective-permute-start.3
  511.8 4.9 collective-permute-start.3
  520.1 4.9 collective-permute-start.3
  528.3 4.9 collective-permute-start.3
  536.6 4.9 collective-permute-start.3
  544.9 4.9 collective-permute-start.3
  (50 other events, 959.7 us)
where the time goes:
time: 558 us; the launch traced here: 551 us
  waiting for transfers between devices  350 us (63%)
  matrix products  86.6 us (16%)
  starting transfers between devices  76.9 us (14%)
  local copies, waits for them, and re-layouts  28.5 us (5%)
  other arithmetic  7.65 us (1%)
    all_to_all x1, waiting for transfers between devices, per_device(): lax.all_to_all(send_keys, 'blk', split_axis=0, concat_axis=0, tiled=True)  167 us
    all_to_all x1, waiting for transfers between devices, per_device(): lax.all_to_all(send_values, 'blk', split_axis=0, concat_axis=0, tiled=True)  166 us
    ppermute x64, starting transfers between devices, shifted(): return lax.ppermute(value, axis, pairs)  60.4 us
    dot_general x16, matrix products, local_partial(): jnp.einsum('rhgd,sthd->rhgst', query_head_rows, key_head_rows, preferred_...  37.1 us
    ppermute x64, waiting for transfers between devices, shifted(): return lax.ppermute(value, axis, pairs)  17.4 us
    dot_general x1, matrix products, per_device(): jnp.einsum('sk,ktw->stw', placing_bf, arrived_values, preferred_element_t...  14.6 us
    dot_general x1, matrix products, per_device(): jnp.einsum('sk,ktw->stw', placing_bf, arrived_keys, preferred_element_typ...  14.3 us
    convert_element_type x1, local copies, waits for them, and re-layouts, per_device(): send_values = jnp.einsum('dqb,btw->dqtw', sending_bf, prefill_values, pre...  11.3 us
  transfers between devices with their start and end apart: 66, of which 34 were waited for; matrix products, arithmetic and copies ran while one was open for 6% of the time, Pallas kernels for 0%

commit v1 on v0

v1 whole, which is shorter than its diff:
```python
import jax
import jax.numpy as jnp
from jax import lax
from jax.experimental import pallas as pl
from jax.experimental.pallas import tpu as pltpu
from jax.sharding import PartitionSpec as P

RANKS = 16
SLOTS = 8
SPILL = 32
REQ = 4
STEPS = 4
COLS = 32
TOK = 128
HEADS = 8
GROUP = 5
DIM = 128
WIDTH = HEADS * DIM
HALF = 64
DATA = 256
TAIL = 48
NEG = -1e30
ANY = pl.BlockSpec(memory_space=pl.ANY)
SMEM = pl.BlockSpec(memory_space=pltpu.SMEM)
VMEM = pl.BlockSpec(memory_space=pltpu.VMEM)
F32 = jnp.float32
BF16 = jnp.bfloat16


def attend_kernel(
    spill, table, lengths, q_ref, ck, cv, pk, pv,
    out_k, out_v, tail_ref,
    inverse, taken, slot_of, kbuf, vbuf, m_s, l_s, o_s, row_s, in_sem, out_sem,
):
    me = lax.axis_index("blk")
    own = SLOTS - 2

    def pre(i):
        return (
            pltpu.make_async_copy(pk.at[i], kbuf.at[own + i], in_sem.at[0, own + i]),
            pltpu.make_async_copy(pv.at[i], vbuf.at[own + i], in_sem.at[1, own + i]),
        )

    def read(e):
        s = slot_of[e]
        return (
            pltpu.make_async_copy(ck.at[s], kbuf.at[e], in_sem.at[0, e]),
            pltpu.make_async_copy(cv.at[s], vbuf.at[e], in_sem.at[1, e]),
        )

    def write(e):
        s = slot_of[e]
        return (
            pltpu.make_async_copy(kbuf.at[e], out_k.at[s], out_sem.at[0, e]),
            pltpu.make_async_copy(vbuf.at[e], out_v.at[s], out_sem.at[1, e]),
        )

    for i in range(2):
        for c in pre(i):
            c.start()
    for s in range(SLOTS):
        taken[s] = 0

    def mark(b, _):
        t = spill[b]

        @pl.when((t >> 3) == me)
        def _():
            taken[t & 7] = 1

        return 0

    lax.fori_loop(0, SPILL, mark, 0)

    def pick(s, n):
        @pl.when(taken[s] == 0)
        def _():
            slot_of[n] = s

        return n + 1 - taken[s]

    lax.fori_loop(0, SLOTS, pick, 0)
    for e in range(own):
        for c in read(e):
            c.start()

    def invert(i, _):
        for r in range(REQ):
            inverse[table[r, i]] = r * COLS + i
        return 0

    lax.fori_loop(0, COLS, invert, 0)
    m_s[...] = jnp.full_like(m_s, NEG)
    l_s[...] = jnp.zeros_like(l_s)
    o_s[...] = jnp.zeros_like(o_s)
    rows = HEADS * 32
    step = (lax.broadcasted_iota(jnp.int32, (rows, TOK), 0) & 31) >> 3
    token = lax.broadcasted_iota(jnp.int32, (rows, TOK), 1) - step

    def visit(e, block):
        place = inverse[block]
        r = place >> 5
        bound = lengths[r] - (place & 31) * TOK - (STEPS - 1)
        visible = token < bound
        s = jnp.concatenate(
            [
                lax.dot_general(
                    q_ref[r, h], kbuf[e, :, h * DIM : (h + 1) * DIM],
                    (((1,), (1,)), ((), ())), preferred_element_type=F32,
                )
                for h in range(HEADS)
            ],
            axis=0,
        ) * (DIM ** -0.5)
        s = jnp.where(visible, s, NEG)
        top = jnp.broadcast_to(jnp.max(s, axis=1, keepdims=True), (rows, TOK))
        old = m_s[r]
        new = jnp.maximum(old, top)
        keep = jnp.exp(old - new)
        w = jnp.where(visible, jnp.exp(s - new), 0.0)
        m_s[r] = new
        l_s[r] = l_s[r] * keep + jnp.sum(w, axis=1, keepdims=True)
        p = w.astype(BF16)
        o = jnp.concatenate(
            [
                jnp.dot(
                    p[h * 32 : (h + 1) * 32], vbuf[e, :, h * DIM : (h + 1) * DIM],
                    preferred_element_type=F32,
                )
                for h in range(HEADS)
            ],
            axis=0,
        )
        o_s[r] = o_s[r] * keep + o

    for i in range(2):
        for c in pre(i):
            c.wait()

    def fresh(i, _):
        visit(own + i, spill[me * 2 + i])
        return 0

    lax.fori_loop(0, 2, fresh, 0)

    def stay(e, _):
        for c in read(e):
            c.wait()
        for c in write(e):
            c.start()
        visit(e, me * SLOTS + slot_of[e])
        return 0

    lax.fori_loop(0, own, stay, 0)

    sub = lax.broadcasted_iota(jnp.int32, (8, DIM), 0)
    lane = lax.broadcasted_iota(jnp.int32, (8, DIM), 1)

    def pack(r, _):
        for a in range(STEPS):
            for h in range(HEADS):
                at = h * 32 + a * 8
                m = m_s[r, at : at + 8, :]
                l = l_s[r, at : at + 8, :]
                hi = l.astype(BF16).astype(F32)
                lo = l - hi
                m_hi = m.astype(BF16).astype(F32)
                m_mid = (m - m_hi).astype(BF16).astype(F32)
                m_lo = m - m_hi - m_mid
                ml = jnp.zeros((8, DIM), F32)
                for n, term in enumerate((m_hi, m_mid, m_lo, hi, lo)):
                    ml = jnp.where(lane == sub + 8 * n, term, ml)
                ml = jnp.sum(ml, axis=0, keepdims=True)
                o = o_s[r, at : at + 8, :]
                row_s[h * 6 : h * 6 + 6, :] = jnp.where(sub == GROUP, ml, o)[:6]
            tail_ref[a * REQ + r] = row_s[...].astype(BF16)
        return 0

    lax.fori_loop(0, REQ, pack, 0)
    for e in range(own):
        for c in write(e):
            c.wait()


def sort_kernel(spill, y, tail, out, count, sem, tail_sem):
    copy = pltpu.make_async_copy(tail, out.at[:, pl.ds(DATA, TAIL)], tail_sem)
    copy.start()
    for k in range(RANKS):
        count[k] = 0

    def send(b, _):
        t = spill[b] >> 3
        n = count[t]
        count[t] = n + 1
        pltpu.make_async_copy(
            y.at[b >> 1, pl.ds(pl.multiple_of((b & 1) * 128, 128), 128)],
            out.at[t, pl.ds(pl.multiple_of(n * 128, 128), 128)],
            sem,
        ).start()
        return 0

    lax.fori_loop(0, SPILL, send, 0)
    pltpu.make_async_copy(y, out.at[:, pl.ds(0, DATA)], sem).wait()
    copy.wait()


def place_kernel(spill, z, key_in, value_in, att, out_k, out_v, slot_of, tail, sem, tail_sem):
    me = lax.axis_index("blk")
    copy = pltpu.make_async_copy(z.at[:, pl.ds(DATA, TAIL)], tail, tail_sem)
    copy.start()

    def find(b, n):
        t = spill[b]
        mine = (t >> 3) == me

        @pl.when(mine)
        def _():
            slot_of[n] = t & 7

        return n + jnp.where(mine, 1, 0)

    lax.fori_loop(0, SPILL, find, 0)
    for q in range(2):
        s = slot_of[q]
        for c in range(RANKS):
            for kv, out in enumerate((out_k, out_v)):
                pltpu.make_async_copy(
                    z.at[c, pl.ds(q * 128 + kv * HALF, HALF)],
                    out.at[s, pl.ds((c % 2) * HALF, HALF), pl.ds((c // 2) * DIM, DIM)],
                    sem,
                ).start()
    copy.wait()
    sub = lax.broadcasted_iota(jnp.int32, (8, DIM), 0)
    lane = lax.broadcasted_iota(jnp.int32, (8, DIM), 1)
    for h in range(HEADS):
        part = [tail[k, h * 6 : h * 6 + 6, :].astype(F32) for k in range(RANKS)]
        ml = jnp.concatenate([x[5:6] for x in part], axis=0)
        peak = ml + (pltpu.roll(ml, DIM - 8, 1) + pltpu.roll(ml, DIM - 16, 1))
        scale = jnp.exp(peak - jnp.max(peak, axis=0, keepdims=True))
        total = pltpu.roll(ml, DIM - 24, 1) + pltpu.roll(ml, DIM - 32, 1)
        down = jnp.sum(scale * total, axis=0, keepdims=True)
        scale = jnp.where(lane[:1] < 8, scale / down, 0.0)
        acc = jnp.zeros((6, DIM), F32)
        for k in range(RANKS):
            col = jnp.sum(jnp.where(lane[:6] == sub[:6], scale[k : k + 1], 0.0), axis=1, keepdims=True)
            acc = acc + col * part[k]
        for g in range(GROUP):
            n = h * GROUP + g
            att[:, n * DIM : (n + 1) * DIM] = acc[g : g + 1].astype(BF16)
    pltpu.make_async_copy(z.at[:, pl.ds(0, DATA)], z.at[:, pl.ds(0, DATA)], sem).wait()


def per_device(queries, cache_keys, values_prior, prefill_keys, prefill_values, lengths, table, spill):
    gathered = lax.all_gather(queries, "blk", axis=0, tiled=True)
    packed = jnp.stack([prefill_keys, prefill_values], axis=1)
    packed = packed.reshape(2, 2, 2, HALF, HEADS, DIM).transpose(4, 2, 0, 1, 3, 5)
    packed = packed.reshape(RANKS, DATA, DIM)
    spread = lax.all_to_all(packed, "blk", split_axis=0, concat_axis=0, tiled=True)

    q = gathered.reshape(STEPS, REQ, HEADS, GROUP, DIM).transpose(1, 2, 0, 3, 4)
    q = jnp.pad(q, ((0, 0), (0, 0), (0, 0), (0, 8 - GROUP), (0, 0))).reshape(REQ, HEADS, 32, DIM)
    pool = jax.ShapeDtypeStruct(cache_keys.shape, BF16)
    rows = HEADS * 32
    keys, values, tail = pl.pallas_call(
        attend_kernel,
        out_shape=(pool, pool, jax.ShapeDtypeStruct((RANKS, TAIL, DIM), BF16)),
        in_specs=[SMEM, SMEM, SMEM, VMEM, ANY, ANY, ANY, ANY],
        out_specs=(ANY, ANY, VMEM),
        scratch_shapes=[
            pltpu.SMEM((RANKS * SLOTS,), jnp.int32),
            pltpu.SMEM((SLOTS,), jnp.int32),
            pltpu.SMEM((SLOTS,), jnp.int32),
            pltpu.VMEM((SLOTS, TOK, WIDTH), BF16),
            pltpu.VMEM((SLOTS, TOK, WIDTH), BF16),
            pltpu.VMEM((REQ, rows, DIM), F32),
            pltpu.VMEM((REQ, rows, DIM), F32),
            pltpu.VMEM((REQ, rows, DIM), F32),
            pltpu.VMEM((TAIL, DIM), F32),
            pltpu.SemaphoreType.DMA((2, SLOTS)),
            pltpu.SemaphoreType.DMA((2, SLOTS)),
        ],
        compiler_params=pltpu.CompilerParams(vmem_limit_bytes=32 << 20),
        cost_estimate=pl.CostEstimate(flops=2 ** 30, bytes_accessed=2 ** 24, transcendentals=2 ** 20),
        name="attend",
    )(spill, table, lengths, q, cache_keys, values_prior, prefill_keys, prefill_values)

    sent = pl.pallas_call(
        sort_kernel,
        out_shape=jax.ShapeDtypeStruct((RANKS, DATA + TAIL, DIM), BF16),
        in_specs=[SMEM, VMEM, VMEM],
        out_specs=ANY,
        scratch_shapes=[pltpu.SMEM((RANKS,), jnp.int32), pltpu.SemaphoreType.DMA, pltpu.SemaphoreType.DMA],
        name="sort",
    )(spill, spread, tail)
    landed = lax.all_to_all(sent, "blk", split_axis=0, concat_axis=0, tiled=True)

    return pl.pallas_call(
        place_kernel,
        out_shape=(jax.ShapeDtypeStruct(queries.shape, BF16), pool, pool),
        in_specs=[SMEM, ANY, ANY, ANY],
        out_specs=(VMEM, ANY, ANY),
        scratch_shapes=[
            pltpu.SMEM((SLOTS,), jnp.int32),
            pltpu.VMEM((RANKS, TAIL, DIM), BF16),
            pltpu.SemaphoreType.DMA,
            pltpu.SemaphoreType.DMA,
        ],
        input_output_aliases={2: 1, 3: 2},
        compiler_params=pltpu.CompilerParams(vmem_limit_bytes=16 << 20),
        name="place",
    )(spill, landed, keys, values)


def solution(mesh):
    both = ("grp", "blk")
    return jax.shard_map(
        per_device,
        mesh=mesh,
        in_specs=(P(both, None), *[P(both, None, None)] * 4, P("grp"), P("grp", None), P("grp")),
        out_specs=(P(both, None), P(both, None, None), P(both, None, None)),
        check_vma=False,
    )
```

time: 558 us -> 107 us (0.19); the launches traced: 551 us -> 106 us
  waiting for transfers between devices: 350 us -> 0.01 us
  matrix products: 86.6 us -> 0 us
  blocking collectives: 0 us -> 76.7 us
  starting transfers between devices: 76.9 us -> 10.3 us
  local copies, waits for them, and re-layouts: 28.5 us -> 4.99 us
  Pallas kernels: 0 us -> 10.9 us
    all_to_all x2 -> x1, waiting for transfers between devices: 332 us -> 0.01 us  [per_device(): lax.all_to_all(packed, 'blk', split_axis=0, concat_axis=0, tiled=True)]
    dot_general x36 -> x0, matrix products: 86.6 us -> none  [the longest x16 37.1 us: local_partial(): jnp.einsum('rhgd,sthd->rhgst', query_head_rows, key_head_rows, preferred_...]
    ppermute x64 -> x0, starting transfers between devices: 60.4 us -> none  [shifted(): return lax.ppermute(value, axis, pairs)]
    all_to_all x0 -> x1, blocking collectives: none -> 38.8 us  [per_device(): lax.all_to_all(sent, 'blk', split_axis=0, concat_axis=0, tiled=True)]
    all_gather x0 -> x1, blocking collectives: none -> 37.9 us  [per_device(): gathered = lax.all_gather(queries, 'blk', axis=0, tiled=True)]
    convert_element_type x3 -> x0, local copies, waits for them, and re-layouts: 23.4 us -> none  [the longest x1 11.3 us: per_device(): send_values = jnp.einsum('dqb,btw->dqtw', sending_bf, prefill_values, pre...]
    ppermute x64 -> x0, waiting for transfers between devices: 17.4 us -> none  [shifted(): return lax.ppermute(value, axis, pairs)]
    pallas_call x0 -> x3, Pallas kernels: none -> 10.9 us  [the longest x1 6.13 us: per_device(): pl.pallas_call(attend_kernel, out_shape=(pool, pool, jax.ShapeDtypeStruct...]
  transfers between devices with their start and end apart: 66 -> 1, of which waited for: 34 -> 0; matrix products, arithmetic and copies ran while one was open for 6% -> 3% of each run, Pallas kernels for 0% -> 6%
where the time goes in v1:
time: 107 us; the launch traced here: 106 us
  blocking collectives  76.7 us (72%)
  Pallas kernels  10.9 us (10%)
  starting transfers between devices  10.3 us (10%)
  local copies, waits for them, and re-layouts  4.99 us (5%)
  other arithmetic  2.73 us (3%)
    all_to_all x1, blocking collectives, per_device(): lax.all_to_all(sent, 'blk', split_axis=0, concat_axis=0, tiled=True)  38.8 us
    all_gather x1, blocking collectives, per_device(): gathered = lax.all_gather(queries, 'blk', axis=0, tiled=True)  37.9 us
    all_to_all x1, starting transfers between devices, per_device(): lax.all_to_all(packed, 'blk', split_axis=0, concat_axis=0, tiled=True)  10.3 us
    pallas_call x1, Pallas kernels, per_device(): pl.pallas_call(attend_kernel, out_shape=(pool, pool, jax.ShapeDtypeStruct...  6.13 us
    unnamed x22, local copies, waits for them, and re-layouts  3.57 us
    pallas_call x1, Pallas kernels, per_device(): pl.pallas_call(place_kernel, out_shape=(jax.ShapeDtypeStruct(queries.shap...  2.38 us
    pallas_call x1, Pallas kernels, per_device(): pl.pallas_call(sort_kernel, out_shape=jax.ShapeDtypeStruct((RANKS, DATA +...  2.37 us
  transfers between devices with their start and end apart: 1, of which 0 were waited for; matrix products, arithmetic and copies ran while one was open for 3% of the time, Pallas kernels for 6%

profile of v1, /device:TPU:1, one launch (start us, length us, event | category | flops | bytes accessed | tf_op | source)
XLA Modules:
  0.0 106.3 jit_solution(1680594337613638763)
XLA Ops:
  0.6 0.0 copy-start.3
  0.6 1.2 %copy.23 = bf16[32,8,8,128]{3,2,1,0:T(8,128)(2,1)S(1)} copy(bf16[32,8,8,128]{3,1,2,0:T(8,128)(2,1)} %bitcast.20) | data formatting | bytes 1048576
  1.8 0.1 copy.19
  2.0 0.0 copy-done.3
  2.0 0.1 copy.22
  2.1 0.1 copy.18
  2.2 0.0 copy-start.9
  2.2 1.1 %pad_maximum_fusion = bf16[2,2,2,64,8,128]{5,3,1,0,2,4:T(8,128)(2,1)} fusion(bf16[2,1,2,64,8,128]{5,3,1,0,2,4:T(8,128)(2,1)S(1)} %copy.19, bf16[2,1,2,64,8,128]{5,3,1,0,2,4:T(8,128)(2,1)S(1)} %copy.18), kind=kLoop, calls=%fused_computation | loop fusion | flops 524288 | bytes 2097152 | tf_op jit(solution)/shard_map/stack | solution.py:255
  3.3 0.0 copy-start.8
  3.3 10.3 %all-to-all-start = ((bf16[16,256,128]{2,1,0:T(8,128)(2,1)}), bf16[16,256,128]{2,1,0:T(8,128)(2,1)}, u32[]{:S(2)}, u32[]{:S(2)}) async-start(bf16[16,256,128]{2,1,0:T(8,128)(2,1)} %bitcast.22), calls=%async_computation | async-start | bytes 2097152 | tf_op jit(solution)/shard_map/all_to_all | solution.py:258
  13.6 0.0 copy-done.9
  13.6 37.9 %all-gather = bf16[16,1,5120]{2,1,0:T(2,128)(2,1)S(1)} all-gather(bf16[1,1,5120]{2,1,0:T(2,128)(2,1)S(1)} %bitcast.25), channel_id=1, replica_groups=mesh['blk'=16,'grp'=16] {'blk'}, dimensions={0}, use_global_device_ids=true | all-gather | bytes 174080 | tf_op jit(solution)/shard_map/all_gather | solution.py:254
  51.4 1.7 %reduce = bf16[16,5120]{1,0:T(8,128)(2,1)} reduce(bf16[16,1,5120]{2,1,0:T(2,128)(2,1)S(1)} %all-gather, bf16[]{:T(256)} %constant.12), dimensions={1}, to_apply=%all-gather.reduce_sub_computation | reduce | bytes 327682 | tf_op jit(solution)/shard_map/all_gather | solution.py:254
  53.1 1.1 %reshape.21 = bf16[4,4,8,5,128]{4,3,2,1,0:T(8,128)(2,1)S(1)} reshape(bf16[16,5120]{1,0:T(8,128)(2,1)} %reduce) | data formatting | bytes 327680 | tf_op jit(solution)/shard_map/reshape | solution.py:260
  54.2 0.1 pad_bitcast_fusion.q_ref
  54.3 0.0 copy-done
  54.3 0.0 copy-start.1
  54.3 1.6 %copy-done.1 = bf16[8,128,1024]{2,1,0:T(8,128)(2,1)S(1)} copy-done((bf16[8,128,1024]{2,1,0:T(8,128)(2,1)S(1)}, bf16[8,128,1024]{2,1,0:T(8,128)(2,1)}, u32[]{:S(2)}) %copy-start.1) | copy-done | bytes 2097176
  55.9 6.1 %attend.1 = (bf16[8,128,1024]{2,1,0:T(8,128)(2,1)}, bf16[8,128,1024]{2,1,0:T(8,128)(2,1)}, bf16[16,48,128]{2,1,0:T(8,128)(2,1)S(1)}) custom-call(s32[32]{0:T(128)S(1)} %copy-done.5, s32[4,32]{1,0:T(4,128)S(1)} %copy-done.7, s32[4]{0:T(128)S(1)} %copy-done.8, bf16[4,8,32,128]{3,2,1,0:T(8,128)(2,1)S(1)} %pad_bitcast_fusion.q_ref, ...), custom_call_target="tpu_custom_call" | custom-call | flops 1073741824 | bytes 16777216 | tf_op jit(solution)/shard_map/attend/pallas_call | solution.py:264
  62.1 0.7 copy-done.4
  62.7 0.0 all-to-all-done.y
  62.7 2.4 %sort.1 = bf16[16,304,128]{2,1,0:T(8,128)(2,1)} custom-call(s32[32]{0:T(128)} %spill.5, bf16[16,256,128]{2,1,0:T(8,128)(2,1)} %all-to-all-done.y, bf16[16,48,128]{2,1,0:T(8,128)(2,1)} %copy-done.4), custom_call_target="tpu_custom_call" | custom-call | tf_op jit(solution)/shard_map/sort/pallas_call | solution.py:287
  65.1 38.8 %all_to_all.10.z = bf16[16,304,128]{2,1,0:T(8,128)(2,1)S(1)} all-to-all(bf16[16,304,128]{2,1,0:T(8,128)(2,1)} %sort.1), channel_id=1, replica_groups=mesh['blk'=16,'grp'=16] {'blk'}, dimensions={0} | all-to-all | bytes 2490368 | tf_op jit(solution)/shard_map/all_to_all | solution.py:295
  104.0 2.4 %place.1 = (bf16[1,5120]{1,0:T(2,128)(2,1)}, bf16[8,128,1024]{2,1,0:T(8,128)(2,1)}, bf16[8,128,1024]{2,1,0:T(8,128)(2,1)}) custom-call(s32[32]{0:T(128)S(1)} %copy-done.6, bf16[16,304,128]{2,1,0:T(8,128)(2,1)S(1)} %all_to_all.10.z, bf16[8,128,1024]{2,1,0:T(8,128)(2,1)} %get-tuple-element.7.key_in, ...), custom_call_target="tpu_custom_call", output_to_operand_aliasing={{1}: (2, {}), {2}: (3, {})} | custom-call | tf_op jit(solution)/shard_map/place/pallas_call | solution.py:297
  (11 shorter events, 0.0 us)
Async XLA Ops:
  0.6 1.3 %copy-start.3 = (bf16[2,128,1024]{2,1,0:T(8,128)(2,1)S(1)}, bf16[2,128,1024]{2,1,0:T(8,128)(2,1)}, u32[]{:S(2)}) copy-start(bf16[2,128,1024]{2,1,0:T(8,128)(2,1)} %pk.1) | copy-start | bytes 1572868
  2.2 11.4 %copy-start.9 = (bf16[1,5120]{1,0:T(2,128)(2,1)S(1)}, bf16[1,5120]{1,0:T(2,128)(2,1)}, u32[]{:S(2)}) copy-start(bf16[1,5120]{1,0:T(2,128)(2,1)} %param.8) | copy-start | bytes 30724
  3.3 51.0 %copy-start = (bf16[8,128,1024]{2,1,0:T(8,128)(2,1)S(1)}, bf16[8,128,1024]{2,1,0:T(8,128)(2,1)}, u32[]{:S(2)}) copy-start(bf16[8,128,1024]{2,1,0:T(8,128)(2,1)} %ck.1) | copy-start | bytes 6291460
  3.3 51.0 %copy-start.2 = (bf16[2,128,1024]{2,1,0:T(8,128)(2,1)S(1)}, bf16[2,128,1024]{2,1,0:T(8,128)(2,1)}, u32[]{:S(2)}) copy-start(bf16[2,128,1024]{2,1,0:T(8,128)(2,1)} %pv.1) | copy-start | bytes 1572868
  3.3 51.0 %copy-start.5 = (s32[32]{0:T(128)S(1)}, s32[32]{0:T(128)}, u32[]{:S(2)}) copy-start(s32[32]{0:T(128)} %spill.5) | copy-start | bytes 388
  3.3 51.0 %copy-start.7 = (s32[4,32]{1,0:T(4,128)S(1)}, s32[4,32]{1,0:T(4,128)}, u32[]{:S(2)}) copy-start(s32[4,32]{1,0:T(4,128)} %table.1) | copy-start | bytes 1540
  3.3 51.0 %copy-start.8 = (s32[4]{0:T(128)S(1)}, s32[4]{0:T(128)}, u32[]{:S(2)}) copy-start(s32[4]{0:T(128)} %lengths.1) | copy-start | bytes 52
  3.3 59.4 %all-to-all-start = ((bf16[16,256,128]{2,1,0:T(8,128)(2,1)}), bf16[16,256,128]{2,1,0:T(8,128)(2,1)}, u32[]{:S(2)}, u32[]{:S(2)}) async-start(bf16[16,256,128]{2,1,0:T(8,128)(2,1)} %bitcast.22), calls=%async_computation | async-start | bytes 2097152 | tf_op jit(solution)/shard_map/all_to_all | solution.py:258
  54.3 1.6 %copy-start.1 = (bf16[8,128,1024]{2,1,0:T(8,128)(2,1)S(1)}, bf16[8,128,1024]{2,1,0:T(8,128)(2,1)}, u32[]{:S(2)}) copy-start(bf16[8,128,1024]{2,1,0:T(8,128)(2,1)} %cv.1) | copy-start | bytes 6291460
  62.1 0.7 copy-start.4
  62.7 41.2 %copy-start.6 = (s32[32]{0:T(128)S(1)}, s32[32]{0:T(128)}, u32[]{:S(2)}) copy-start(s32[32]{0:T(128)} %spill.5) | copy-start | bytes 388

commit v2 on v1

v2 whole, which is shorter than its diff:
```python
import jax
import jax.numpy as jnp
from jax import lax
from jax.experimental import pallas as pl
from jax.experimental.pallas import tpu as pltpu
from jax.sharding import PartitionSpec as P

RANKS = 16
SLOTS = 8
KEPT = 6
SPILL = 32
REQ = 4
STEPS = 4
COLS = 32
TOK = 128
HEADS = 8
GROUP = 5
DIM = 128
WIDTH = HEADS * DIM
HALF = 64
DATA = 256
TAIL = 48
LENGTHS = 32
TABLE = 64
REQUEST = 32
BOUND = 40
HOME = 48
PLAN = 64
NEG = -1e30
ANY = pl.BlockSpec(memory_space=pl.ANY)
SMEM = pl.BlockSpec(memory_space=pltpu.SMEM)
VMEM = pl.BlockSpec(memory_space=pltpu.VMEM)
HBM = pl.BlockSpec(memory_space=pltpu.HBM)
DMA = pltpu.SemaphoreType.DMA
F32 = jnp.float32
BF16 = jnp.bfloat16


def pack_kernel(q, pk, pv, out, q_in, q_rows, buf, q_sem, sem):
    get = pltpu.make_async_copy(q, q_in, q_sem)
    get.start()
    loads = []
    for b in range(2):
        for kv, source in enumerate((pk, pv)):
            for half in range(2):
                n = b * 4 + kv * 2 + half
                loads.append(pltpu.make_async_copy(source.at[b, pl.ds(half * HALF, HALF)], buf.at[n], sem.at[n]))
                loads[-1].start()
    q_rows[...] = jnp.zeros_like(q_rows)
    get.wait()
    for n in range(HEADS * GROUP):
        q_rows[n : n + 1, :] = q_in[:, n * DIM : (n + 1) * DIM].astype(F32)
    q_bf = q_rows[...].astype(BF16)
    for k in range(RANKS):
        out[k, DATA:, :] = q_bf
    for n, load in enumerate(loads):
        load.wait()
        at = (n >> 1) * HALF
        for h in range(HEADS):
            out[2 * h + (n & 1), at : at + HALF, :] = buf[n, :, h * DIM : (h + 1) * DIM]


def load_kernel(
    ints, ck, cv, pk, pv, out_k, out_v, reads_out, plan,
    inverse, taken, slot_of, count, buf, in_sem, out_sem, get_sem,
):
    me = lax.axis_index("blk")
    reads, writes = [], []
    for i in range(2):
        for kv, source in enumerate((pk, pv)):
            e = KEPT + i
            reads.append(pltpu.make_async_copy(source.at[i], buf.at[kv, e], in_sem.at[kv, e]))
            writes.append([pltpu.make_async_copy(buf.at[kv, e], reads_out.at[kv, e], get_sem.at[kv, e])])
            reads[-1].start()
    for s in range(SLOTS):
        taken[s] = 0
    for k in range(RANKS):
        count[k] = 0
    for k in range(PLAN):
        plan[k] = 0

    def mark(b, _):
        slot = ints[b]
        t = slot >> 3
        n = count[t]
        count[t] = n + 1
        plan[b] = t * 2 + n

        @pl.when(t == me)
        def _():
            taken[slot & 7] = 1
            plan[HOME + n] = slot & 7

        return 0

    lax.fori_loop(0, SPILL, mark, 0)

    def pick(s, n):
        @pl.when(taken[s] == 0)
        def _():
            slot_of[n] = s

        return n + 1 - taken[s]

    lax.fori_loop(0, SLOTS, pick, 0)
    for e in range(KEPT):
        s = slot_of[e]
        for kv, (source, out) in enumerate(((ck, out_k), (cv, out_v))):
            reads.append(pltpu.make_async_copy(source.at[s], buf.at[kv, e], in_sem.at[kv, e]))
            writes.append([
                pltpu.make_async_copy(buf.at[kv, e], reads_out.at[kv, e], get_sem.at[kv, e]),
                pltpu.make_async_copy(buf.at[kv, e], out.at[s], out_sem.at[kv, e]),
            ])
            reads[-1].start()

    def invert(i, _):
        for r in range(REQ):
            inverse[ints[TABLE + r * COLS + i]] = r * COLS + i
        return 0

    lax.fori_loop(0, COLS, invert, 0)
    for e in range(SLOTS):
        place = inverse[me * SLOTS + slot_of[e] if e < KEPT else ints[me * 2 + (e - KEPT)]]
        plan[REQUEST + e] = place >> 5
        plan[BOUND + e] = ints[LENGTHS + (place >> 5)] - (place & 31) * TOK - (STEPS - 1)
    for r, w in zip(reads, writes):
        r.wait()
        for c in w:
            c.start()
    for w in writes:
        for c in w:
            c.wait()


def attend_kernel(
    plan, spread, blocks, sent, kbuf, vbuf, q_rows, q_s, s_buf, top_s, m_s, l_s, o_s, row_s, sem
):
    order = tuple(range(SLOTS))
    loads = {}
    for e in order:
        for kv, buf in enumerate((kbuf, vbuf)):
            loads[e, kv] = pltpu.make_async_copy(blocks.at[kv, e], buf.at[e], sem.at[kv, e])
    for kv in range(2):
        for e in order:
            loads[e, kv].start()
    m_s[...] = jnp.full_like(m_s, NEG)
    l_s[...] = jnp.zeros_like(l_s)
    o_s[...] = jnp.zeros_like(o_s)
    q_s[...] = jnp.zeros_like(q_s)
    request = [plan[REQUEST + e] for e in range(SLOTS)]
    bound = [plan[BOUND + e] for e in range(SLOTS)]
    for i in range(RANKS):
        a, r = i // REQ, i % REQ
        q_rows[i] = spread[i, DATA:, :].astype(F32)
        for h in range(HEADS):
            q_s[r, h, a * 8 : a * 8 + GROUP, :] = q_rows[i, h * GROUP : (h + 1) * GROUP, :]
    rows = HEADS * 32
    step = (lax.broadcasted_iota(jnp.int32, (rows, TOK), 0) & 31) >> 3
    token = lax.broadcasted_iota(jnp.int32, (rows, TOK), 1) - step
    for n, e in enumerate(order):
        if n % 2 == 0:
            loads[order[n], 0].wait()
            loads[order[n + 1], 0].wait()
        s = jnp.concatenate(
            [
                lax.dot_general(
                    q_s[request[e], h].astype(BF16), kbuf[e, :, h * DIM : (h + 1) * DIM],
                    (((1,), (1,)), ((), ())), preferred_element_type=F32,
                )
                for h in range(HEADS)
            ],
            axis=0,
        ) * (DIM ** -0.5)
        s = jnp.where(token < bound[e], s, NEG)
        s_buf[e] = s
        top_s[e] = jnp.broadcast_to(jnp.max(s, axis=1, keepdims=True), (rows, TOK))
    for b in range(SPILL):
        to = plan[b]
        sent[to >> 1, pl.ds(pl.multiple_of((to & 1) * 128, 128), 128), :] = spread[
            b >> 1, (b & 1) * 128 : (b & 1) * 128 + 128, :
        ]
    for e in range(SLOTS):
        m_s[request[e]] = jnp.maximum(m_s[request[e]], top_s[e])
    for n, e in enumerate(order):
        if n % 4 == 0:
            for other in order[n : n + 4]:
                loads[other, 1].wait()
        w = jnp.where(token < bound[e], jnp.exp(s_buf[e] - m_s[request[e]]), 0.0)
        p = w.astype(BF16)
        o = jnp.concatenate(
            [
                jnp.dot(
                    p[h * 32 : (h + 1) * 32], vbuf[e, :, h * DIM : (h + 1) * DIM],
                    preferred_element_type=F32,
                )
                for h in range(HEADS)
            ],
            axis=0,
        )
        top_s[e] = jnp.broadcast_to(jnp.sum(w, axis=1, keepdims=True), (rows, TOK))
        s_buf[e] = o
    for e in range(SLOTS):
        l_s[request[e]] = l_s[request[e]] + top_s[e]
        o_s[request[e]] = o_s[request[e]] + s_buf[e]

    sub = lax.broadcasted_iota(jnp.int32, (8, DIM), 0)
    lane = lax.broadcasted_iota(jnp.int32, (8, DIM), 1)
    for r in range(REQ):
        for a in range(STEPS):
            for h in range(HEADS):
                at = h * 32 + a * 8
                row_s[r, a, h * GROUP : (h + 1) * GROUP, :] = o_s[r, at : at + GROUP, :]
                ml = jnp.where(lane == sub, m_s[r, at : at + 8, :], 0.0)
                ml = jnp.where(lane == sub + 8, l_s[r, at : at + 8, :], ml)
                row_s[r, a, 40 + h : 41 + h, :] = jnp.sum(ml, axis=0, keepdims=True)
            ml = row_s[r, a, 40:, :]
            hi = ml.astype(BF16).astype(F32)
            mid = (ml - hi).astype(BF16).astype(F32)
            row_s[r, a, 40:, :] = hi + pltpu.roll(mid, 16, 1) + pltpu.roll(ml - hi - mid, 32, 1)
            sent[a * REQ + r, DATA:, :] = row_s[r, a].astype(BF16)


def place_kernel(plan, z, key_in, value_in, att, out_k, out_v, tail, sem):
    for n in range(2):
        slot = plan[HOME + n]
        for c in range(RANKS):
            for kv, out in enumerate((out_k, out_v)):
                pltpu.make_async_copy(
                    z.at[c, pl.ds(n * 128 + kv * HALF, HALF)],
                    out.at[slot, pl.ds((c % 2) * HALF, HALF), pl.ds((c // 2) * DIM, DIM)],
                    sem,
                ).start()
    for k in range(RANKS):
        tail[k] = z[k, DATA:, :].astype(F32)
    sub = lax.broadcasted_iota(jnp.int32, (8, DIM), 0)
    lane = lax.broadcasted_iota(jnp.int32, (8, DIM), 1)
    state = []
    for k in range(RANKS):
        ml = tail[k, 40:, :]
        state.append(ml + (pltpu.roll(ml, DIM - 16, 1) + pltpu.roll(ml, DIM - 32, 1)))
    top = state[0]
    for x in state[1:]:
        top = jnp.maximum(top, x)
    scales = [jnp.exp(x - top) for x in state]
    down = jnp.zeros((8, DIM), F32)
    for x, scale in zip(state, scales):
        down = down + scale * pltpu.roll(x, DIM - 8, 1)
    inverse = jnp.where(lane < GROUP, 1.0 / jnp.where(lane < GROUP, down, 1.0), 0.0)
    scales = [jnp.where(lane < GROUP, scale, 0.0) * inverse for scale in scales]
    for h in range(HEADS):
        acc = jnp.zeros((GROUP, DIM), F32)
        for k in range(RANKS):
            col = jnp.sum(jnp.where(lane == sub, scales[k][h : h + 1], 0.0), axis=1, keepdims=True)
            acc = acc + col[:GROUP] * tail[k, h * GROUP : (h + 1) * GROUP, :]
        for g in range(GROUP):
            n = h * GROUP + g
            att[:, n * DIM : (n + 1) * DIM] = acc[g : g + 1].astype(BF16)
    pltpu.make_async_copy(z.at[:, pl.ds(0, DATA)], z.at[:, pl.ds(0, DATA)], sem).wait()


def per_device(queries, cache_keys, values_prior, prefill_keys, prefill_values, lengths, table, spill):
    pool = jax.ShapeDtypeStruct(cache_keys.shape, BF16)
    message = jax.ShapeDtypeStruct((RANKS, DATA + TAIL, DIM), BF16)
    rows = HEADS * 32
    ints = jnp.concatenate([spill, lengths, jnp.zeros((TABLE - LENGTHS - REQ,), jnp.int32), table.reshape(-1)])
    packed = pl.pallas_call(
        pack_kernel,
        out_shape=message,
        in_specs=[HBM] * 3,
        out_specs=VMEM,
        scratch_shapes=[
            pltpu.VMEM(queries.shape, BF16),
            pltpu.VMEM((TAIL, DIM), F32),
            pltpu.VMEM((8, HALF, WIDTH), BF16),
            DMA,
            DMA((8,)),
        ],
        compiler_params=pltpu.CompilerParams(vmem_limit_bytes=59 << 20),
        name="pack",
    )(queries, prefill_keys, prefill_values)
    spread = lax.all_to_all(packed, "blk", split_axis=0, concat_axis=0, tiled=True)

    keys, values, blocks, plan = pl.pallas_call(
        load_kernel,
        out_shape=(
            pool,
            pool,
            jax.ShapeDtypeStruct((2, SLOTS, TOK, WIDTH), BF16),
            jax.ShapeDtypeStruct((PLAN,), jnp.int32),
        ),
        in_specs=[SMEM] + [HBM] * 4,
        out_specs=(HBM, HBM, HBM, SMEM),
        scratch_shapes=[
            pltpu.SMEM((RANKS * SLOTS,), jnp.int32),
            pltpu.SMEM((SLOTS,), jnp.int32),
            pltpu.SMEM((SLOTS,), jnp.int32),
            pltpu.SMEM((RANKS,), jnp.int32),
            pltpu.VMEM((2, SLOTS, TOK, WIDTH), BF16),
            DMA((2, SLOTS)),
            DMA((2, SLOTS)),
            DMA((2, SLOTS)),
        ],
        compiler_params=pltpu.CompilerParams(vmem_limit_bytes=58 << 20),
        cost_estimate=pl.CostEstimate(flops=0, bytes_accessed=7 << 20, transcendentals=0),
        name="load",
    )(ints, cache_keys, values_prior, prefill_keys, prefill_values)

    sent = pl.pallas_call(
        attend_kernel,
        out_shape=message,
        in_specs=[SMEM, VMEM, HBM],
        out_specs=VMEM,
        scratch_shapes=[
            pltpu.VMEM((SLOTS, TOK, WIDTH), BF16),
            pltpu.VMEM((SLOTS, TOK, WIDTH), BF16),
            pltpu.VMEM((RANKS, TAIL, DIM), F32),
            pltpu.VMEM((REQ, HEADS, 32, DIM), F32),
            pltpu.VMEM((SLOTS, rows, DIM), F32),
            pltpu.VMEM((SLOTS, rows, DIM), F32),
            pltpu.VMEM((REQ, rows, DIM), F32),
            pltpu.VMEM((REQ, rows, DIM), F32),
            pltpu.VMEM((REQ, rows, DIM), F32),
            pltpu.VMEM((REQ, STEPS, TAIL, DIM), F32),
            DMA((2, SLOTS)),
        ],
        compiler_params=pltpu.CompilerParams(vmem_limit_bytes=50 << 20),
        cost_estimate=pl.CostEstimate(flops=2 ** 29, bytes_accessed=2 ** 23, transcendentals=2 ** 18),
        name="attend",
    )(plan, spread, blocks)
    landed = lax.all_to_all(sent, "blk", split_axis=0, concat_axis=0, tiled=True)

    return pl.pallas_call(
        place_kernel,
        out_shape=(jax.ShapeDtypeStruct(queries.shape, BF16), pool, pool),
        in_specs=[SMEM, VMEM, HBM, HBM],
        out_specs=(VMEM, HBM, HBM),
        scratch_shapes=[pltpu.VMEM((RANKS, TAIL, DIM), F32), DMA],
        input_output_aliases={2: 1, 3: 2},
        compiler_params=pltpu.CompilerParams(vmem_limit_bytes=16 << 20),
        name="place",
    )(plan, landed, keys, values)


def solution(mesh):
    both = ("grp", "blk")
    return jax.shard_map(
        per_device,
        mesh=mesh,
        in_specs=(P(both, None), *[P(both, None, None)] * 4, P("grp"), P("grp", None), P("grp")),
        out_specs=(P(both, None), P(both, None, None), P(both, None, None)),
        check_vma=False,
    )
```

time: 107 us -> 89.3 us (0.83)
  blocking collectives: 76.7 us -> 36.4 us
  waiting for transfers between devices: 0.01 us -> 25.4 us
  local copies, waits for them, and re-layouts: 4.99 us -> 0.75 us
  Pallas kernels: 10.9 us -> 15.1 us
  other arithmetic: 2.73 us -> 0.64 us
    all_gather x1 -> x0, blocking collectives: 37.9 us -> none  [per_device(): gathered = lax.all_gather(queries, 'blk', axis=0, tiled=True)]
    all_to_all x1, waiting for transfers between devices: 0.01 us -> 25.4 us  [per_device(): lax.all_to_all(packed, 'blk', split_axis=0, concat_axis=0, tiled=True)]
    pallas_call x2 -> x3, Pallas kernels: 8.5 us -> 13 us  [the longest x1 5.72 us: per_device(): pl.pallas_call(load_kernel, out_shape=(pool, pool, jax.ShapeDtypeStruct((...]
    unnamed x22 -> x8, local copies, waits for them, and re-layouts: 3.57 us -> 0.67 us
    all_to_all x1, blocking collectives: 38.8 us -> 36.4 us  [per_device(): lax.all_to_all(sent, 'blk', split_axis=0, concat_axis=0, tiled=True)]
    all_gather x1 -> x0, other arithmetic: 1.66 us -> none  [per_device(): gathered = lax.all_gather(queries, 'blk', axis=0, tiled=True)]
    reshape x2 -> x1, local copies, waits for them, and re-layouts: 1.19 us -> 0.08 us  [per_device(): table.reshape(-1)]
    another operation x1 -> x0, other arithmetic: 1.07 us -> none  [per_device(): packed = jnp.stack([prefill_keys, prefill_values], axis=1)]
  transfers between devices with their start and end apart: 1 -> 1, of which waited for: 0 -> 1; matrix products, arithmetic and copies ran while one was open for 3% -> 1% of each run, Pallas kernels for 6% -> 6%
where the time goes in v2:
time: 89.3 us; the launch traced here: 89 us
  blocking collectives  36.4 us (41%)
  waiting for transfers between devices  25.4 us (28%)
  Pallas kernels  15.1 us (17%)
  starting transfers between devices  9.99 us (11%)
    all_to_all x1, blocking collectives, per_device(): lax.all_to_all(sent, 'blk', split_axis=0, concat_axis=0, tiled=True)  36.4 us
    all_to_all x1, waiting for transfers between devices, per_device(): lax.all_to_all(packed, 'blk', split_axis=0, concat_axis=0, tiled=True)  25.4 us
    all_to_all x1, starting transfers between devices, per_device(): lax.all_to_all(packed, 'blk', split_axis=0, concat_axis=0, tiled=True)  9.99 us
    pallas_call x1, Pallas kernels, per_device(): pl.pallas_call(load_kernel, out_shape=(pool, pool, jax.ShapeDtypeStruct((...  5.72 us
    pallas_call x1, Pallas kernels, per_device(): pl.pallas_call(attend_kernel, out_shape=message, in_specs=[SMEM, VMEM, HB...  4.82 us
    pallas_call x1, Pallas kernels, per_device(): pl.pallas_call(pack_kernel, out_shape=message, in_specs=[HBM] * 3, out_sp...  2.46 us
    pallas_call x1, Pallas kernels, per_device(): pl.pallas_call(place_kernel, out_shape=(jax.ShapeDtypeStruct(queries.shap...  2.15 us
  transfers between devices with their start and end apart: 1, of which 1 were waited for; matrix products, arithmetic and copies ran while one was open for 1% of the time, Pallas kernels for 6%

profile of v2, /device:TPU:1, one launch (start us, length us, event | category | flops | bytes accessed | tf_op | source)
XLA Modules:
  0.0 89.0 jit_solution(17104720394993430423)
XLA Ops:
  0.6 0.0 copy-start.1
  0.6 0.0 copy-start.3
  0.7 0.0 copy-start.2
  0.7 2.5 %pack.1 = bf16[16,304,128]{2,1,0:T(8,128)(2,1)} custom-call(bf16[1,5120]{1,0:T(2,128)(2,1)} %q.1, bf16[2,128,1024]{2,1,0:T(8,128)(2,1)} %pk.3, bf16[2,128,1024]{2,1,0:T(8,128)(2,1)} %pv.3), custom_call_target="tpu_custom_call" | custom-call | tf_op jit(solution)/shard_map/pack/pallas_call | solution.py:266
  3.1 10.0 %all-to-all-start = ((bf16[16,304,128]{2,1,0:T(8,128)(2,1)}), bf16[16,304,128]{2,1,0:T(8,128)(2,1)S(1)}, u32[]{:S(2)}, u32[]{:S(2)}) async-start(bf16[16,304,128]{2,1,0:T(8,128)(2,1)} %pack.1), calls=%async_computation | async-start | bytes 2490368 | tf_op jit(solution)/shard_map/all_to_all | solution.py:281
  13.1 0.0 copy-done.1
  13.1 0.1 reshape.9
  13.2 0.0 copy-done.3
  13.2 0.0 copy-done.2
  13.2 0.6 pad_add_fusion.ints
  13.9 5.7 %load.1 = (bf16[8,128,1024]{2,1,0:T(8,128)(2,1)}, bf16[8,128,1024]{2,1,0:T(8,128)(2,1)}, bf16[2,8,128,1024]{3,2,1,0:T(8,128)(2,1)}, s32[64]{0:T(128)}) custom-call(s32[192]{0:T(256)} %pad_add_fusion.ints, bf16[8,128,1024]{2,1,0:T(8,128)(2,1)} %ck.1, bf16[8,128,1024]{2,1,0:T(8,128)(2,1)} %cv.1, bf16[2,128,1024]{2,1,0:T(8,128)(2,1)} %pk.3, ...), custom_call_target="tpu_custom_call" | custom-call | bytes 7340032 | tf_op jit(solution)/shard_map/load/pallas_call | solution.py:283
  19.6 25.4 %all-to-all-done.spread = bf16[16,304,128]{2,1,0:T(8,128)(2,1)S(1)} async-done(((bf16[16,304,128]{2,1,0:T(8,128)(2,1)}), bf16[16,304,128]{2,1,0:T(8,128)(2,1)S(1)}, u32[]{:S(2)}, u32[]{:S(2)}) %all-to-all-start) | async-done | bytes 1245216 | tf_op jit(solution)/shard_map/all_to_all | solution.py:281
  45.0 0.0 copy-start
  45.0 0.7 copy-done
  45.7 4.8 %attend.1 = bf16[16,304,128]{2,1,0:T(8,128)(2,1)S(1)} custom-call(s32[64]{0:T(128)S(1)} %copy-done, bf16[16,304,128]{2,1,0:T(8,128)(2,1)S(1)} %all-to-all-done.spread, bf16[2,8,128,1024]{3,2,1,0:T(8,128)(2,1)} %get-tuple-element.8.blocks), custom_call_target="tpu_custom_call" | custom-call | flops 536870912 | bytes 8388608 | tf_op jit(solution)/shard_map/attend/pallas_call | solution.py:308
  50.5 36.4 %all_to_all.10.z = bf16[16,304,128]{2,1,0:T(8,128)(2,1)S(1)} all-to-all(bf16[16,304,128]{2,1,0:T(8,128)(2,1)S(1)} %attend.1), channel_id=1, replica_groups=mesh['blk'=16,'grp'=16] {'blk'}, dimensions={0} | all-to-all | bytes 2490368 | tf_op jit(solution)/shard_map/all_to_all | solution.py:330
  86.8 2.1 %place.1 = (bf16[1,5120]{1,0:T(2,128)(2,1)}, bf16[8,128,1024]{2,1,0:T(8,128)(2,1)}, bf16[8,128,1024]{2,1,0:T(8,128)(2,1)}) custom-call(s32[64]{0:T(128)S(1)} %copy-done, bf16[16,304,128]{2,1,0:T(8,128)(2,1)S(1)} %all_to_all.10.z, bf16[8,128,1024]{2,1,0:T(8,128)(2,1)} %get-tuple-element.9.key_in, ...), custom_call_target="tpu_custom_call", output_to_operand_aliasing={{1}: (2, {}), {2}: (3, {})} | custom-call | tf_op jit(solution)/shard_map/place/pallas_call | solution.py:332
  (1 shorter events, 0.0 us)
Async XLA Ops:
  0.6 12.5 %copy-start.1 = (s32[4,32]{1,0:T(4,128)S(1)}, s32[4,32]{1,0:T(4,128)}, u32[]{:S(2)}) copy-start(s32[4,32]{1,0:T(4,128)} %param.14) | copy-start | bytes 1540
  0.6 12.6 %copy-start.3 = (s32[32]{0:T(128)S(1)}, s32[32]{0:T(128)}, u32[]{:S(2)}) copy-start(s32[32]{0:T(128)} %param.15) | copy-start | bytes 388
  0.7 12.6 %copy-start.2 = (s32[4]{0:T(128)S(1)}, s32[4]{0:T(128)}, u32[]{:S(2)}) copy-start(s32[4]{0:T(128)} %param.13) | copy-start | bytes 52
  3.1 41.9 %all-to-all-start = ((bf16[16,304,128]{2,1,0:T(8,128)(2,1)}), bf16[16,304,128]{2,1,0:T(8,128)(2,1)S(1)}, u32[]{:S(2)}, u32[]{:S(2)}) async-start(bf16[16,304,128]{2,1,0:T(8,128)(2,1)} %pack.1), calls=%async_computation | async-start | bytes 2490368 | tf_op jit(solution)/shard_map/all_to_all | solution.py:281
  45.0 0.7 copy-start

commit v3 on v2

--- a/solution.py
+++ b/solution.py
@@ -25,7 +25,8 @@
 REQUEST = 32
 BOUND = 40
 HOME = 48
-PLAN = 64
+PLAN = 128
+FAR = 1 << 22
 NEG = -1e30
 ANY = pl.BlockSpec(memory_space=pl.ANY)
 SMEM = pl.BlockSpec(memory_space=pltpu.SMEM)
@@ -36,33 +37,44 @@
 BF16 = jnp.bfloat16
 
 
-def pack_kernel(q, pk, pv, out, q_in, q_rows, buf, q_sem, sem):
-    get = pltpu.make_async_copy(q, q_in, q_sem)
-    get.start()
-    loads = []
+def pack_kernel(q, pk, pv, out, q_in, q_rows, buf, stage, q_sem, sem, out_sem):
+    loads, stores = [], []
     for b in range(2):
         for kv, source in enumerate((pk, pv)):
             for half in range(2):
                 n = b * 4 + kv * 2 + half
                 loads.append(pltpu.make_async_copy(source.at[b, pl.ds(half * HALF, HALF)], buf.at[n], sem.at[n]))
                 loads[-1].start()
+    get = pltpu.make_async_copy(q, q_in, q_sem)
+    get.start()
+    for n in range(4):
+        part = pl.ds(n * HALF, HALF)
+        stores.append(pltpu.make_async_copy(stage.at[:, part], out.at[:, part], out_sem.at[n]))
+    part = pl.ds(DATA, TAIL)
+    stores.append(pltpu.make_async_copy(stage.at[:, part], out.at[:, part], out_sem.at[4]))
     q_rows[...] = jnp.zeros_like(q_rows)
-    get.wait()
-    for n in range(HEADS * GROUP):
-        q_rows[n : n + 1, :] = q_in[:, n * DIM : (n + 1) * DIM].astype(F32)
-    q_bf = q_rows[...].astype(BF16)
-    for k in range(RANKS):
-        out[k, DATA:, :] = q_bf
     for n, load in enumerate(loads):
         load.wait()
         at = (n >> 1) * HALF
         for h in range(HEADS):
-            out[2 * h + (n & 1), at : at + HALF, :] = buf[n, :, h * DIM : (h + 1) * DIM]
+            stage[2 * h + (n & 1), at : at + HALF, :] = buf[n, :, h * DIM : (h + 1) * DIM]
+        if n % 2 == 1:
+            stores[n >> 1].start()
+        if n == 3:
+            get.wait()
+            for m in range(HEADS * GROUP):
+                q_rows[m : m + 1, :] = q_in[:, m * DIM : (m + 1) * DIM].astype(F32)
+            q_bf = q_rows[...].astype(BF16)
+            for k in range(RANKS):
+                stage[k, DATA:, :] = q_bf
+            stores[4].start()
+    for c in stores:
+        c.wait()
 
 
 def load_kernel(
-    ints, ck, cv, pk, pv, out_k, out_v, reads_out, plan,
-    inverse, taken, slot_of, count, buf, in_sem, out_sem, get_sem,
+    ints, ck, cv, pk, pv, out_k, out_v, reads_out, plan, far,
+    inverse, taken, slot_of, count, buf, in_sem, out_sem, get_sem, far_sem,
 ):
     me = lax.axis_index("blk")
     reads, writes = [], []
@@ -123,6 +135,8 @@
         place = inverse[me * SLOTS + slot_of[e] if e < KEPT else ints[me * 2 + (e - KEPT)]]
         plan[REQUEST + e] = place >> 5
         plan[BOUND + e] = ints[LENGTHS + (place >> 5)] - (place & 31) * TOK - (STEPS - 1)
+    copy = pltpu.make_async_copy(plan, far.at[pl.ds(0, PLAN)], far_sem)
+    copy.start()
     for r, w in zip(reads, writes):
         r.wait()
         for c in w:
@@ -130,11 +144,14 @@
     for w in writes:
         for c in w:
             c.wait()
+    copy.wait()
 
 
 def attend_kernel(
-    plan, spread, blocks, sent, kbuf, vbuf, q_rows, q_s, s_buf, top_s, m_s, l_s, o_s, row_s, sem
+    far, spread, blocks, sent, plan, kbuf, vbuf, q_rows, q_s, s_buf, top_s, m_s, l_s, o_s, row_s, sem, plan_sem
 ):
+    copy = pltpu.make_async_copy(far.at[pl.ds(0, PLAN)], plan, plan_sem)
+    copy.start()
     order = tuple(range(SLOTS))
     loads = {}
     for e in order:
@@ -147,13 +164,14 @@
     l_s[...] = jnp.zeros_like(l_s)
     o_s[...] = jnp.zeros_like(o_s)
     q_s[...] = jnp.zeros_like(q_s)
-    request = [plan[REQUEST + e] for e in range(SLOTS)]
-    bound = [plan[BOUND + e] for e in range(SLOTS)]
     for i in range(RANKS):
         a, r = i // REQ, i % REQ
         q_rows[i] = spread[i, DATA:, :].astype(F32)
         for h in range(HEADS):
             q_s[r, h, a * 8 : a * 8 + GROUP, :] = q_rows[i, h * GROUP : (h + 1) * GROUP, :]
+    copy.wait()
+    request = [plan[REQUEST + e] for e in range(SLOTS)]
+    bound = [plan[BOUND + e] for e in range(SLOTS)]
     rows = HEADS * 32
     step = (lax.broadcasted_iota(jnp.int32, (rows, TOK), 0) & 31) >> 3
     token = lax.broadcasted_iota(jnp.int32, (rows, TOK), 1) - step
@@ -267,29 +285,32 @@
         pack_kernel,
         out_shape=message,
         in_specs=[HBM] * 3,
-        out_specs=VMEM,
+        out_specs=HBM,
         scratch_shapes=[
             pltpu.VMEM(queries.shape, BF16),
             pltpu.VMEM((TAIL, DIM), F32),
             pltpu.VMEM((8, HALF, WIDTH), BF16),
+            pltpu.VMEM(message.shape, BF16),
             DMA,
             DMA((8,)),
+            DMA((5,)),
         ],
         compiler_params=pltpu.CompilerParams(vmem_limit_bytes=59 << 20),
         name="pack",
     )(queries, prefill_keys, prefill_values)
     spread = lax.all_to_all(packed, "blk", split_axis=0, concat_axis=0, tiled=True)
 
-    keys, values, blocks, plan = pl.pallas_call(
+    keys, values, blocks, plan, far = pl.pallas_call(
         load_kernel,
         out_shape=(
             pool,
             pool,
             jax.ShapeDtypeStruct((2, SLOTS, TOK, WIDTH), BF16),
             jax.ShapeDtypeStruct((PLAN,), jnp.int32),
+            jax.ShapeDtypeStruct((FAR,), jnp.int32),
         ),
         in_specs=[SMEM] + [HBM] * 4,
-        out_specs=(HBM, HBM, HBM, SMEM),
+        out_specs=(HBM, HBM, HBM, SMEM, HBM),
         scratch_shapes=[
             pltpu.SMEM((RANKS * SLOTS,), jnp.int32),
             pltpu.SMEM((SLOTS,), jnp.int32),
@@ -299,6 +320,7 @@
             DMA((2, SLOTS)),
             DMA((2, SLOTS)),
             DMA((2, SLOTS)),
+            DMA,
         ],
         compiler_params=pltpu.CompilerParams(vmem_limit_bytes=58 << 20),
         cost_estimate=pl.CostEstimate(flops=0, bytes_accessed=7 << 20, transcendentals=0),
@@ -308,9 +330,10 @@
     sent = pl.pallas_call(
         attend_kernel,
         out_shape=message,
-        in_specs=[SMEM, VMEM, HBM],
+        in_specs=[HBM, VMEM, HBM],
         out_specs=VMEM,
         scratch_shapes=[
+            pltpu.SMEM((PLAN,), jnp.int32),
             pltpu.VMEM((SLOTS, TOK, WIDTH), BF16),
             pltpu.VMEM((SLOTS, TOK, WIDTH), BF16),
             pltpu.VMEM((RANKS, TAIL, DIM), F32),
@@ -322,11 +345,12 @@
             pltpu.VMEM((REQ, rows, DIM), F32),
             pltpu.VMEM((REQ, STEPS, TAIL, DIM), F32),
             DMA((2, SLOTS)),
+            DMA,
         ],
         compiler_params=pltpu.CompilerParams(vmem_limit_bytes=50 << 20),
         cost_estimate=pl.CostEstimate(flops=2 ** 29, bytes_accessed=2 ** 23, transcendentals=2 ** 18),
         name="attend",
-    )(plan, spread, blocks)
+    )(far, spread, blocks)
     landed = lax.all_to_all(sent, "blk", split_axis=0, concat_axis=0, tiled=True)
 
     return pl.pallas_call(

time: 89.3 us -> 87.9 us (0.984)
  transfers between devices with their start and end apart: 1 -> 1, of which waited for: 1 -> 1; matrix products, arithmetic and copies ran while one was open for 1% -> 1% of each run, Pallas kernels for 6% -> 7%
where the time goes in v3:
time: 87.9 us; the launch traced here: 87.6 us
  blocking collectives  36.4 us (41%)
  waiting for transfers between devices  25.3 us (29%)
  Pallas kernels  14.5 us (16%)
  starting transfers between devices  9.99 us (11%)
    all_to_all x1, blocking collectives, per_device(): lax.all_to_all(sent, 'blk', split_axis=0, concat_axis=0, tiled=True)  36.4 us
    all_to_all x1, waiting for transfers between devices, per_device(): lax.all_to_all(packed, 'blk', split_axis=0, concat_axis=0, tiled=True)  25.3 us
    all_to_all x1, starting transfers between devices, per_device(): lax.all_to_all(packed, 'blk', split_axis=0, concat_axis=0, tiled=True)  9.99 us
    pallas_call x1, Pallas kernels, per_device(): pl.pallas_call(load_kernel, out_shape=(pool, pool, jax.ShapeDtypeStruct((...  5.84 us
    pallas_call x1, Pallas kernels, per_device(): pl.pallas_call(attend_kernel, out_shape=message, in_specs=[HBM, VMEM, HBM...  4.29 us
    pallas_call x1, Pallas kernels, per_device(): pl.pallas_call(pack_kernel, out_shape=message, in_specs=[HBM] * 3, out_sp...  2.24 us
    pallas_call x1, Pallas kernels, per_device(): pl.pallas_call(place_kernel, out_shape=(jax.ShapeDtypeStruct(queries.shap...  2.15 us
  transfers between devices with their start and end apart: 1, of which 1 were waited for; matrix products, arithmetic and copies ran while one was open for 1% of the time, Pallas kernels for 7%

profile of v3, /device:TPU:1, one launch (start us, length us, event | category | flops | bytes accessed | tf_op | source)
XLA Modules:
  0.0 87.6 jit_solution(2485950803184729048)
XLA Ops:
  0.6 0.0 copy-start.1
  0.6 0.0 copy-start.3
  0.7 0.0 copy-start.2
  0.7 2.2 %pack.1 = bf16[16,304,128]{2,1,0:T(8,128)(2,1)} custom-call(bf16[1,5120]{1,0:T(2,128)(2,1)} %q.1, bf16[2,128,1024]{2,1,0:T(8,128)(2,1)} %pk.3, bf16[2,128,1024]{2,1,0:T(8,128)(2,1)} %pv.3), custom_call_target="tpu_custom_call" | custom-call | tf_op jit(solution)/shard_map/pack/pallas_call | solution.py:284
  2.9 10.0 %all-to-all-start = ((bf16[16,304,128]{2,1,0:T(8,128)(2,1)}), bf16[16,304,128]{2,1,0:T(8,128)(2,1)S(1)}, u32[]{:S(2)}, u32[]{:S(2)}) async-start(bf16[16,304,128]{2,1,0:T(8,128)(2,1)} %pack.1), calls=%async_computation | async-start | bytes 2490368 | tf_op jit(solution)/shard_map/all_to_all | solution.py:301
  12.9 0.0 copy-done.1
  12.9 0.1 reshape.9
  13.0 0.0 copy-done.3
  13.0 0.0 copy-done.2
  13.0 0.6 pad_add_fusion.ints
  13.6 5.8 %load.1 = (bf16[8,128,1024]{2,1,0:T(8,128)(2,1)}, bf16[8,128,1024]{2,1,0:T(8,128)(2,1)}, bf16[2,8,128,1024]{3,2,1,0:T(8,128)(2,1)}, s32[128]{0:T(128)}, s32[4194304]{0:T(1024)}) custom-call(s32[192]{0:T(256)} %pad_add_fusion.ints, bf16[8,128,1024]{2,1,0:T(8,128)(2,1)} %ck.1, bf16[8,128,1024]{2,1,0:T(8,128)(2,1)} %cv.1, bf16[2,128,1024]{2,1,0:T(8,128)(2,1)} %pk.3, ...), custom_call_target="tpu_custom_call" | custom-call | bytes 7340032 | tf_op jit(solution)/shard_map/load/pallas_call | solution.py:303
  19.5 25.3 %all-to-all-done.spread = bf16[16,304,128]{2,1,0:T(8,128)(2,1)S(1)} async-done(((bf16[16,304,128]{2,1,0:T(8,128)(2,1)}), bf16[16,304,128]{2,1,0:T(8,128)(2,1)S(1)}, u32[]{:S(2)}, u32[]{:S(2)}) %all-to-all-start) | async-done | bytes 1245216 | tf_op jit(solution)/shard_map/all_to_all | solution.py:301
  44.8 4.3 %attend.1 = bf16[16,304,128]{2,1,0:T(8,128)(2,1)S(1)} custom-call(s32[4194304]{0:T(1024)} %get-tuple-element.9.far, bf16[16,304,128]{2,1,0:T(8,128)(2,1)S(1)} %all-to-all-done.spread, bf16[2,8,128,1024]{3,2,1,0:T(8,128)(2,1)} %get-tuple-element.10.blocks), custom_call_target="tpu_custom_call" | custom-call | flops 536870912 | bytes 8388608 | tf_op jit(solution)/shard_map/attend/pallas_call | solution.py:330
  49.1 0.0 copy-start
  49.1 36.4 %all_to_all.10.z = bf16[16,304,128]{2,1,0:T(8,128)(2,1)S(1)} all-to-all(bf16[16,304,128]{2,1,0:T(8,128)(2,1)S(1)} %attend.1), channel_id=1, replica_groups=mesh['blk'=16,'grp'=16] {'blk'}, dimensions={0} | all-to-all | bytes 2490368 | tf_op jit(solution)/shard_map/all_to_all | solution.py:354
  85.4 0.0 copy-done
  85.5 2.1 %place.1 = (bf16[1,5120]{1,0:T(2,128)(2,1)}, bf16[8,128,1024]{2,1,0:T(8,128)(2,1)}, bf16[8,128,1024]{2,1,0:T(8,128)(2,1)}) custom-call(s32[128]{0:T(128)S(1)} %copy-done, bf16[16,304,128]{2,1,0:T(8,128)(2,1)S(1)} %all_to_all.10.z, bf16[8,128,1024]{2,1,0:T(8,128)(2,1)} %get-tuple-element.11.key_in, ...), custom_call_target="tpu_custom_call", output_to_operand_aliasing={{1}: (2, {}), {2}: (3, {})} | custom-call | tf_op jit(solution)/shard_map/place/pallas_call | solution.py:356
  (1 shorter events, 0.0 us)
Async XLA Ops:
  0.6 12.3 %copy-start.1 = (s32[4,32]{1,0:T(4,128)S(1)}, s32[4,32]{1,0:T(4,128)}, u32[]{:S(2)}) copy-start(s32[4,32]{1,0:T(4,128)} %param.14) | copy-start | bytes 1540
  0.6 12.4 %copy-start.3 = (s32[32]{0:T(128)S(1)}, s32[32]{0:T(128)}, u32[]{:S(2)}) copy-start(s32[32]{0:T(128)} %param.15) | copy-start | bytes 388
  0.7 12.3 %copy-start.2 = (s32[4]{0:T(128)S(1)}, s32[4]{0:T(128)}, u32[]{:S(2)}) copy-start(s32[4]{0:T(128)} %param.13) | copy-start | bytes 52
  2.9 41.9 %all-to-all-start = ((bf16[16,304,128]{2,1,0:T(8,128)(2,1)}), bf16[16,304,128]{2,1,0:T(8,128)(2,1)S(1)}, u32[]{:S(2)}, u32[]{:S(2)}) async-start(bf16[16,304,128]{2,1,0:T(8,128)(2,1)} %pack.1), calls=%async_computation | async-start | bytes 2490368 | tf_op jit(solution)/shard_map/all_to_all | solution.py:301
  49.1 36.4 %copy-start = (s32[128]{0:T(128)S(1)}, s32[128]{0:T(128)}, u32[]{:S(2)}) copy-start(s32[128]{0:T(128)} %get-tuple-element.8.plan) | copy-start | bytes 1540

commit v4 on v3

--- a/solution.py
+++ b/solution.py
@@ -148,7 +148,7 @@
 
 
 def attend_kernel(
-    far, spread, blocks, sent, plan, kbuf, vbuf, q_rows, q_s, s_buf, top_s, m_s, l_s, o_s, row_s, sem, plan_sem
+    far, spread, blocks, sent, plan, kbuf, vbuf, q_rows, q_s, s_buf, top_s, m_s, l_s, o_s, row_s, p_s, sem, plan_sem
 ):
     copy = pltpu.make_async_copy(far.at[pl.ds(0, PLAN)], plan, plan_sem)
     copy.start()
@@ -199,12 +199,17 @@
         ]
     for e in range(SLOTS):
         m_s[request[e]] = jnp.maximum(m_s[request[e]], top_s[e])
+    for e in order:
+        w = jnp.where(token < bound[e], jnp.exp(s_buf[e] - m_s[request[e]]), 0.0)
+        p_s[e] = w.astype(BF16)
+        top_s[e] = jnp.broadcast_to(jnp.sum(w, axis=1, keepdims=True), (rows, TOK))
+    for e in order:
+        l_s[request[e]] = l_s[request[e]] + top_s[e]
     for n, e in enumerate(order):
         if n % 4 == 0:
             for other in order[n : n + 4]:
                 loads[other, 1].wait()
-        w = jnp.where(token < bound[e], jnp.exp(s_buf[e] - m_s[request[e]]), 0.0)
-        p = w.astype(BF16)
+        p = p_s[e]
         o = jnp.concatenate(
             [
                 jnp.dot(
@@ -215,10 +220,8 @@
             ],
             axis=0,
         )
-        top_s[e] = jnp.broadcast_to(jnp.sum(w, axis=1, keepdims=True), (rows, TOK))
         s_buf[e] = o
     for e in range(SLOTS):
-        l_s[request[e]] = l_s[request[e]] + top_s[e]
         o_s[request[e]] = o_s[request[e]] + s_buf[e]
 
     sub = lax.broadcasted_iota(jnp.int32, (8, DIM), 0)
@@ -344,6 +347,7 @@
             pltpu.VMEM((REQ, rows, DIM), F32),
             pltpu.VMEM((REQ, rows, DIM), F32),
             pltpu.VMEM((REQ, STEPS, TAIL, DIM), F32),
+            pltpu.VMEM((SLOTS, rows, TOK), BF16),
             DMA((2, SLOTS)),
             DMA,
         ],

time: 87.9 us -> 88.1 us (level)
  no operation moved by 1% of the time
where the time goes in v4:
time: 88.1 us; the launch traced here: 87.8 us
  blocking collectives  36.4 us (41%)
  waiting for transfers between devices  25.3 us (29%)
  Pallas kernels  14.7 us (17%)
  starting transfers between devices  9.99 us (11%)
    all_to_all x1, blocking collectives, per_device(): lax.all_to_all(sent, 'blk', split_axis=0, concat_axis=0, tiled=True)  36.4 us
    all_to_all x1, waiting for transfers between devices, per_device(): lax.all_to_all(packed, 'blk', split_axis=0, concat_axis=0, tiled=True)  25.3 us
    all_to_all x1, starting transfers between devices, per_device(): lax.all_to_all(packed, 'blk', split_axis=0, concat_axis=0, tiled=True)  9.99 us
    pallas_call x1, Pallas kernels, per_device(): pl.pallas_call(load_kernel, out_shape=(pool, pool, jax.ShapeDtypeStruct((...  5.84 us
    pallas_call x1, Pallas kernels, per_device(): pl.pallas_call(attend_kernel, out_shape=message, in_specs=[HBM, VMEM, HBM...  4.48 us
    pallas_call x1, Pallas kernels, per_device(): pl.pallas_call(pack_kernel, out_shape=message, in_specs=[HBM] * 3, out_sp...  2.24 us
    pallas_call x1, Pallas kernels, per_device(): pl.pallas_call(place_kernel, out_shape=(jax.ShapeDtypeStruct(queries.shap...  2.15 us
  transfers between devices with their start and end apart: 1, of which 1 were waited for; matrix products, arithmetic and copies ran while one was open for 1% of the time, Pallas kernels for 7%

profile of v4, /device:TPU:1, one launch (start us, length us, event | category | flops | bytes accessed | tf_op | source)
XLA Modules:
  0.0 87.8 jit_solution(352358213175484783)
XLA Ops:
  0.6 0.0 copy-start.1
  0.6 0.0 copy-start.3
  0.7 0.0 copy-start.2
  0.7 2.2 %pack.1 = bf16[16,304,128]{2,1,0:T(8,128)(2,1)} custom-call(bf16[1,5120]{1,0:T(2,128)(2,1)} %q.1, bf16[2,128,1024]{2,1,0:T(8,128)(2,1)} %pk.3, bf16[2,128,1024]{2,1,0:T(8,128)(2,1)} %pv.3), custom_call_target="tpu_custom_call" | custom-call | tf_op jit(solution)/shard_map/pack/pallas_call | solution.py:287
  2.9 10.0 %all-to-all-start = ((bf16[16,304,128]{2,1,0:T(8,128)(2,1)}), bf16[16,304,128]{2,1,0:T(8,128)(2,1)S(1)}, u32[]{:S(2)}, u32[]{:S(2)}) async-start(bf16[16,304,128]{2,1,0:T(8,128)(2,1)} %pack.1), calls=%async_computation | async-start | bytes 2490368 | tf_op jit(solution)/shard_map/all_to_all | solution.py:304
  12.9 0.0 copy-done.1
  12.9 0.1 reshape.9
  13.0 0.0 copy-done.3
  13.0 0.0 copy-done.2
  13.0 0.6 pad_add_fusion.ints
  13.6 5.8 %load.1 = (bf16[8,128,1024]{2,1,0:T(8,128)(2,1)}, bf16[8,128,1024]{2,1,0:T(8,128)(2,1)}, bf16[2,8,128,1024]{3,2,1,0:T(8,128)(2,1)}, s32[128]{0:T(128)}, s32[4194304]{0:T(1024)}) custom-call(s32[192]{0:T(256)} %pad_add_fusion.ints, bf16[8,128,1024]{2,1,0:T(8,128)(2,1)} %ck.1, bf16[8,128,1024]{2,1,0:T(8,128)(2,1)} %cv.1, bf16[2,128,1024]{2,1,0:T(8,128)(2,1)} %pk.3, ...), custom_call_target="tpu_custom_call" | custom-call | bytes 7340032 | tf_op jit(solution)/shard_map/load/pallas_call | solution.py:306
  19.5 25.3 %all-to-all-done.spread = bf16[16,304,128]{2,1,0:T(8,128)(2,1)S(1)} async-done(((bf16[16,304,128]{2,1,0:T(8,128)(2,1)}), bf16[16,304,128]{2,1,0:T(8,128)(2,1)S(1)}, u32[]{:S(2)}, u32[]{:S(2)}) %all-to-all-start) | async-done | bytes 1245216 | tf_op jit(solution)/shard_map/all_to_all | solution.py:304
  44.8 4.5 %attend.1 = bf16[16,304,128]{2,1,0:T(8,128)(2,1)S(1)} custom-call(s32[4194304]{0:T(1024)} %get-tuple-element.9.far, bf16[16,304,128]{2,1,0:T(8,128)(2,1)S(1)} %all-to-all-done.spread, bf16[2,8,128,1024]{3,2,1,0:T(8,128)(2,1)} %get-tuple-element.10.blocks), custom_call_target="tpu_custom_call" | custom-call | flops 536870912 | bytes 8388608 | tf_op jit(solution)/shard_map/attend/pallas_call | solution.py:333
  49.3 0.0 copy-start
  49.3 36.4 %all_to_all.10.z = bf16[16,304,128]{2,1,0:T(8,128)(2,1)S(1)} all-to-all(bf16[16,304,128]{2,1,0:T(8,128)(2,1)S(1)} %attend.1), channel_id=1, replica_groups=mesh['blk'=16,'grp'=16] {'blk'}, dimensions={0} | all-to-all | bytes 2490368 | tf_op jit(solution)/shard_map/all_to_all | solution.py:358
  85.6 0.0 copy-done
  85.6 2.1 %place.1 = (bf16[1,5120]{1,0:T(2,128)(2,1)}, bf16[8,128,1024]{2,1,0:T(8,128)(2,1)}, bf16[8,128,1024]{2,1,0:T(8,128)(2,1)}) custom-call(s32[128]{0:T(128)S(1)} %copy-done, bf16[16,304,128]{2,1,0:T(8,128)(2,1)S(1)} %all_to_all.10.z, bf16[8,128,1024]{2,1,0:T(8,128)(2,1)} %get-tuple-element.11.key_in, ...), custom_call_target="tpu_custom_call", output_to_operand_aliasing={{1}: (2, {}), {2}: (3, {})} | custom-call | tf_op jit(solution)/shard_map/place/pallas_call | solution.py:360
  (1 shorter events, 0.0 us)
Async XLA Ops:
  0.6 12.3 %copy-start.1 = (s32[4,32]{1,0:T(4,128)S(1)}, s32[4,32]{1,0:T(4,128)}, u32[]{:S(2)}) copy-start(s32[4,32]{1,0:T(4,128)} %param.14) | copy-start | bytes 1540
  0.6 12.4 %copy-start.3 = (s32[32]{0:T(128)S(1)}, s32[32]{0:T(128)}, u32[]{:S(2)}) copy-start(s32[32]{0:T(128)} %param.15) | copy-start | bytes 388
  0.7 12.3 %copy-start.2 = (s32[4]{0:T(128)S(1)}, s32[4]{0:T(128)}, u32[]{:S(2)}) copy-start(s32[4]{0:T(128)} %param.13) | copy-start | bytes 52
  2.9 41.9 %all-to-all-start = ((bf16[16,304,128]{2,1,0:T(8,128)(2,1)}), bf16[16,304,128]{2,1,0:T(8,128)(2,1)S(1)}, u32[]{:S(2)}, u32[]{:S(2)}) async-start(bf16[16,304,128]{2,1,0:T(8,128)(2,1)} %pack.1), calls=%async_computation | async-start | bytes 2490368 | tf_op jit(solution)/shard_map/all_to_all | solution.py:304
  49.3 36.4 %copy-start = (s32[128]{0:T(128)S(1)}, s32[128]{0:T(128)}, u32[]{:S(2)}) copy-start(s32[128]{0:T(128)} %get-tuple-element.8.plan) | copy-start | bytes 1540
